TPU v7x, 128 devices: a whole 4x4x4 slice. The times are simulated.
128 devices in a mesh: gx: 8 (over z, core), gy: 16 (over y, x).
Axes of the slice: x: 4, y: 4, z: 4, core: 2. Of those that a mesh axis runs over, the one named last changes fastest.
Arguments:
- displacement: float32 [3, 24, 384, 384], P(None, 'gx', 'gy'), may hold values from -1.6015 to 1.6015, as said below
- velocity: float32 [3, 24, 384, 384], P(None, 'gx', 'gy'), may hold values from -6 to 6
- energy: float32 [27, 8, 128, 128], P(None, 'gx', 'gy'), may hold values from 0.5 to 18
- mass_weight: float32 [216, 8, 128, 128], P(None, 'gx', 'gy'), may hold values from 0.002 to 0.02
- pinned_flags: int32 [3, 24, 384, 384], P(None, 'gx', 'gy'), may hold values 0 or 1
Outputs:
- acceleration: float32 [3, 24, 384, 384], P(None, 'gx', 'gy')
- velocity_new: float32 [3, 24, 384, 384], P(None, 'gx', 'gy')
- displacement_new: float32 [3, 24, 384, 384], P(None, 'gx', 'gy')
- energy_new: float32 [27, 8, 128, 128], P(None, 'gx', 'gy')
Inputs may be any that keep to these rules, and one draw needn't show every extreme that they name: Every entry of the displacement's derivative along local element coordinates stays below 0.11 in magnitude.
All inputs are finite; a program needn't handle non-finite values. No bound on the sum of `pinned_flags` on one device may be relied on, other than what follows from the above.
Results may differ from a plain program's by a relative error of at most 0.00018.
Values sent between devices are 32-bit elements; how exact they have to be, the bound alone decides.
No kernel may reach another device: no remote copies, remote signals or barrier semaphores. Data moves between devices by JAX's collectives and lax.ppermute only.
A program may use at most 128 MiB of HBM per device.

v0:
```python
from functools import partial
import math
import jax
import jax.numpy as jnp
import numpy as np
from jax import lax
from jax.sharding import PartitionSpec as P

Q = 6
ITERS = 3
HIGHEST = lax.Precision.HIGHEST
step_size = 0.05
viscosity = 0.3
gamma_less = 0.4


def shifted_2(shard, axis, by):
    devices = lax.axis_size(axis)
    return lax.ppermute(shard, axis, [(i, (i + by) % devices) for i in range(devices)])


def basis_tables():
    root_five = 1.0 / math.sqrt(5.0)
    lobatto = np.array([0.0, 0.5 - 0.5 * root_five, 0.5 + 0.5 * root_five, 1.0])
    legendre = np.array(
        [
            -0.932469514203152,
            -0.6612093864662645,
            -0.2386191860831909,
            0.2386191860831909,
            0.6612093864662645,
            0.932469514203152,
        ]
    )
    abscissa = 0.5 + 0.5 * legendre
    shape_values = np.ones((6, 4))
    shape_slopes = np.zeros((6, 4))
    for a in range(4):
        for b in range(4):
            if b != a:
                shape_values[:, a] = (
                    shape_values[:, a] * (abscissa - lobatto[b]) / (lobatto[a] - lobatto[b])
                )
        for c in range(4):
            if c != a:
                factor_term = np.ones(6) / (lobatto[a] - lobatto[c])
                for b in range(4):
                    if b != a and b != c:
                        factor_term = (
                            factor_term * (abscissa - lobatto[b]) / (lobatto[a] - lobatto[b])
                        )
                shape_slopes[:, a] = shape_slopes[:, a] + factor_term
    thermo_values = np.stack(
        [
            (1.0 - abscissa) * (1.0 - abscissa),
            2.0 * abscissa * (1.0 - abscissa),
            abscissa * abscissa,
        ],
        axis=1,
    )
    return (
        jnp.asarray(shape_values, jnp.float32),
        jnp.asarray(shape_slopes, jnp.float32),
        jnp.asarray(thermo_values, jnp.float32),
    )


def along_x(matrix, operand):
    return jnp.einsum("qa,cabgjk->cqbgjk", matrix, operand, precision=HIGHEST)


def along_y(matrix, operand):
    return jnp.einsum("qb,cabgjk->caqgjk", matrix, operand, precision=HIGHEST)


def along_z(matrix, operand):
    return jnp.einsum("qg,cabgjk->cabqjk", matrix, operand, precision=HIGHEST)


def split_nodes(operand, which_axis):
    num_cells = (operand.shape[which_axis] - 1) // 3
    outer_dims = operand.shape[:which_axis]
    inner_dims = operand.shape[which_axis + 1 :]
    head_part = lax.slice_in_dim(operand, 0, 3 * num_cells, axis=which_axis).reshape(
        outer_dims + (num_cells, 3) + inner_dims
    )
    head_part = jnp.moveaxis(head_part, which_axis + 1, which_axis)
    tail_part = lax.slice_in_dim(operand, 3, 3 * num_cells + 1, stride=3, axis=which_axis)
    return jnp.concatenate([head_part, jnp.expand_dims(tail_part, which_axis)], axis=which_axis)


def merge_nodes(operand, which_axis):
    num_cells = operand.shape[which_axis + 1]
    outer_dims = operand.shape[:which_axis]
    inner_dims = operand.shape[which_axis + 2 :]
    head_part = jnp.moveaxis(
        lax.slice_in_dim(operand, 0, 3, axis=which_axis), which_axis, which_axis + 1
    )
    head_part = head_part.reshape(outer_dims + (3 * num_cells,) + inner_dims)
    tail_part = jnp.moveaxis(
        lax.slice_in_dim(operand, 3, 4, axis=which_axis), which_axis, which_axis + 1
    )
    pad_tail = [(0, 0)] * tail_part.ndim
    pad_tail[which_axis + 1] = (0, 2)
    tail_part = jnp.pad(tail_part, pad_tail).reshape(outer_dims + (3 * num_cells,) + inner_dims)
    pad_head = [(0, 0)] * head_part.ndim
    pad_head[which_axis] = (0, 1)
    pad_shift = [(0, 0)] * head_part.ndim
    pad_shift[which_axis] = (3, 0)
    shifted = lax.slice_in_dim(jnp.pad(tail_part, pad_shift), 0, 3 * num_cells + 1, axis=which_axis)
    return jnp.pad(head_part, pad_head) + shifted


def slab_elements(slab_field):
    closed = jnp.concatenate([slab_field, slab_field[..., :1]], axis=-1)
    parts_y = split_nodes(closed, 2)
    parts_z = split_nodes(parts_y, 4)
    return jnp.moveaxis(parts_z, 4, 3)


def slab_assemble(element_field):
    parts_z = merge_nodes(jnp.moveaxis(element_field, 3, 4), 4)
    parts_y = merge_nodes(parts_z, 2)
    return jnp.concatenate([parts_y[..., :1] + parts_y[..., -1:], parts_y[..., 1:-1]], axis=-1)


def over_blocks(node_fields, cell_data, element_fn):
    num_cells = cell_data[0].shape[1]

    def one_block(block_index):
        node_start = 3 * block_index
        element_sets = tuple(
            (
                slab_elements(lax.dynamic_slice_in_dim(field_in, node_start, 4, axis=1))
                for field_in in node_fields
            )
        )
        cell_block = tuple(
            (
                lax.dynamic_index_in_dim(member, block_index, axis=1, keepdims=False)
                for member in cell_data
            )
        )
        contribution, outputs_extra = element_fn(element_sets, cell_block)
        return (slab_assemble(contribution), outputs_extra)

    node_pieces, extra_parts = lax.map(one_block, jnp.arange(num_cells, dtype=jnp.int32))
    assembled = merge_nodes(jnp.moveaxis(node_pieces, 0, 2), 1)
    return (assembled, tuple((jnp.moveaxis(member, 0, 1) for member in extra_parts)))


def thermo_interp(thermo_values, dofs):
    return along_x(thermo_values, along_y(thermo_values, along_z(thermo_values, dofs[None])))[0]


def thermo_project(thermo_values, at_quad):
    moved = thermo_values.T
    return along_x(moved, along_y(moved, along_z(moved, at_quad[None])))[0]


def force_block(element_sets, cell_block, basis_set):
    shape_values, shape_slopes, thermo_values = basis_set
    kinematic = element_sets[0]
    energy_block, weight_block = cell_block
    trailing_shape = energy_block.shape[1:]
    z_values = along_z(shape_values, kinematic)
    z_slopes = along_z(shape_slopes, kinematic)
    yz_values = along_y(shape_values, z_values)
    gradients = [
        along_x(shape_slopes, yz_values),
        along_x(shape_values, along_y(shape_slopes, z_values)),
        along_x(shape_values, along_y(shape_values, z_slopes)),
    ]
    jacobian = [[gradients[d][c] + (1.0 if c == d else 0.0) for d in range(3)] for c in range(3)]
    grad_vel = [[gradients[d][3 + c] for d in range(3)] for c in range(3)]
    cofactor = [
        [
            jacobian[(c + 1) % 3][(d + 1) % 3] * jacobian[(c + 2) % 3][(d + 2) % 3]
            - jacobian[(c + 1) % 3][(d + 2) % 3] * jacobian[(c + 2) % 3][(d + 1) % 3]
            for d in range(3)
        ]
        for c in range(3)
    ]
    determinant = (
        jacobian[0][0] * cofactor[0][0]
        + jacobian[0][1] * cofactor[0][1]
        + jacobian[0][2] * cofactor[0][2]
    )
    inverse_det = 1.0 / determinant
    spatial_grad = [
        [
            (
                grad_vel[c][0] * cofactor[e][0]
                + grad_vel[c][1] * cofactor[e][1]
                + grad_vel[c][2] * cofactor[e][2]
            )
            * inverse_det
            for e in range(3)
        ]
        for c in range(3)
    ]
    energy_quad = thermo_interp(thermo_values, energy_block.reshape((3, 3, 3) + trailing_shape))
    mass_quad = weight_block.reshape((Q, Q, Q) + trailing_shape)
    scale_quad = mass_quad * inverse_det
    stress_shape = [
        [
            viscosity * (spatial_grad[c][d] + spatial_grad[d][c])
            - (gamma_less * energy_quad if c == d else 0.0)
            for d in range(3)
        ]
        for c in range(3)
    ]
    flux = [
        [
            scale_quad
            * (
                stress_shape[c][0] * cofactor[0][f]
                + stress_shape[c][1] * cofactor[1][f]
                + stress_shape[c][2] * cofactor[2][f]
            )
            for f in range(3)
        ]
        for c in range(3)
    ]
    power_quad = jnp.zeros_like(mass_quad)
    for c in range(3):
        for f in range(3):
            power_quad = power_quad + flux[c][f] * grad_vel[c][f]
    flux_cols = [jnp.stack([flux[c][f] for c in range(3)]) for f in range(3)]
    moved = along_x(shape_slopes.T, along_y(shape_values.T, along_z(shape_values.T, flux_cols[0])))
    moved = moved + along_x(
        shape_values.T,
        along_y(shape_slopes.T, along_z(shape_values.T, flux_cols[1]))
        + along_y(shape_values.T, along_z(shape_slopes.T, flux_cols[2])),
    )
    energy_rhs = thermo_project(thermo_values, power_quad)
    lumped_mass = thermo_project(thermo_values, mass_quad)
    energy_next = energy_block + step_size * (energy_rhs / lumped_mass).reshape(energy_block.shape)
    return (-moved, (energy_next,))


def mass_block(element_sets, cell_block, basis_set):
    shape_values = basis_set[0]
    mass_quad = cell_block[0].reshape((Q, Q, Q) + cell_block[0].shape[1:])
    at_quad = (
        along_x(shape_values, along_y(shape_values, along_z(shape_values, element_sets[0])))
        * mass_quad
    )
    return (along_x(shape_values.T, along_y(shape_values.T, along_z(shape_values.T, at_quad))), ())


def extend_right(field_in):
    right_rim = shifted_2(field_in[:, :1], "gx", -1)
    wide_field = jnp.concatenate([field_in, right_rim], axis=1)
    top_rim = shifted_2(wide_field[:, :, :1], "gy", -1)
    return jnp.concatenate([wide_field, top_rim], axis=2)


def fold_back(field_in):
    upper_rim = shifted_2(field_in[:, :, -1:], "gy", 1)
    field_in = jnp.concatenate([field_in[:, :, :1] + upper_rim, field_in[:, :, 1:-1]], axis=2)
    side_rim = shifted_2(field_in[:, -1:], "gx", 1)
    return jnp.concatenate([field_in[:, :1] + side_rim, field_in[:, 1:-1]], axis=1)


def global_sum(value):
    return lax.psum(value, ("gx", "gy"))


def on_device(displacement, velocity, energy, mass_weight, pinned_flags):
    basis_set = basis_tables()
    free_mask = (1 - pinned_flags).astype(jnp.float32)
    kinematic = jnp.concatenate([displacement, velocity], axis=0)
    mass_apply = partial(mass_block, basis_set=basis_set)
    rows_x = displacement.shape[1]
    rows_y = displacement.shape[2]
    assembled, extra_parts = over_blocks(
        (extend_right(kinematic),), (energy, mass_weight), partial(force_block, basis_set=basis_set)
    )
    nodal_force = fold_back(assembled)
    owned = 1.0
    residual = free_mask * nodal_force
    energy_new = extra_parts[0]

    def local_inner(first, second):
        return jnp.sum(owned * (first * second))

    acceleration = jnp.zeros_like(residual)
    direction = residual
    norm_now = global_sum(local_inner(residual, residual))
    for iteration in range(ITERS):
        contribution = over_blocks((extend_right(direction),), (mass_weight,), mass_apply)[0]
        mass_image = free_mask * fold_back(contribution)
        step_length = norm_now / global_sum(local_inner(direction, mass_image))
        acceleration = acceleration + step_length * direction
        residual = residual - step_length * mass_image
        norm_next = global_sum(local_inner(residual, residual))
        direction = residual + norm_next / norm_now * direction
        norm_now = norm_next
    acceleration = acceleration[:, :rows_x, :rows_y]
    velocity_new = velocity + step_size * acceleration
    displacement_new = displacement + step_size * velocity_new
    return (acceleration, velocity_new, displacement_new, energy_new)


def solution(mesh):
    in_specs = (
        P(None, "gx", "gy", None),
        P(None, "gx", "gy", None),
        P(None, "gx", "gy", None),
        P(None, "gx", "gy", None),
        P(None, "gx", "gy", None),
    )
    out_specs = (
        P(None, "gx", "gy", None),
        P(None, "gx", "gy", None),
        P(None, "gx", "gy", None),
        P(None, "gx", "gy", None),
    )
    return jax.shard_map(
        on_device, mesh=mesh, in_specs=in_specs, out_specs=out_specs, check_vma=False
    )
```

profile of v0, /device:TPU:1, one launch (start us, length us, event | category | flops | bytes accessed | tf_op | source)
XLA Modules:
  0.0 1001.1 jit_solution(13770269630577380290)
XLA Ops:
  21.4 12.5 %copy.282 = f32[6,4,4,8,384]{3,2,4,1,0:T(4,128)} copy(f32[6,4,4,8,384]{4,3,2,1,0:T(8,128)S(1)} %fusion.109) | data formatting | bytes 2359296 | tf_op jit(solution)/shard_map/while/body/eval_jaxpr/slice | solution.py:84
  33.9 18.3 %copy.283 = f32[6,4,4,8,128,3]{4,5,3,2,1,0:T(4,128)S(1)} copy(f32[6,4,4,8,128,3]{3,2,5,4,1,0:T(4,128)} %bitcast.311) | data formatting | bytes 2359296 | tf_op jit(solution)/shard_map/while/body/eval_jaxpr/reshape | solution.py:84
  52.2 15.2 %slice.434 = f32[6,4,4,8,128]{4,3,2,1,0:T(8,128)S(1)} slice(f32[6,4,4,8,385]{4,3,2,1,0:T(8,128)} %pad_maximum_fusion.3), slice={[0:6:1], [0:4:1], [0:4:1], [0:8:1], [3:385:3]} | slice | bytes 786432 | tf_op jit(solution)/shard_map/while/body/eval_jaxpr/slice | solution.py:88
  86.1 9.3 fusion.18
  101.1 9.5 fusion.16
  110.6 9.5 fusion.20
  121.0 10.7 %copy_bitcast_fusion = (f32[6,6,6,6,8,128]{5,4,3,2,1,0:T(8,128)}, f32[6,6,6,6,8,128]{5,4,3,2,1,0:T(8,128)}) fusion(f32[6,6,6,8,128,6]{4,5,3,2,1,0:T(8,128)} %fusion.16, f32[6,6,6,8,128,6]{4,5,3,2,1,0:T(8,128)} %fusion.18), kind=kLoop, calls=%fused_computation.12 | loop fusion | bytes 21233664 | tf_op jit(solution)/shard_map/while/body/eval_jaxpr/qa,cabgjk->cqbgjk/transpose | solution.py:69
  144.5 11.0 %add_bitcast_fusion = (f32[6,6,6,8,128]{4,3,2,1,0:T(8,128)}, f32[1,6,6,6,8,128]{5,4,3,2,1,0:T(8,128)}, f32[1,6,6,6,8,128]{5,4,3,2,1,0:T(8,128)}, f32[1,6,6,6,8,1...) fusion(f32[1,6,6,6,8,128]{5,4,3,2,1,0:T(8,128)S(1)} %get-tuple-, ...), kind=kLoop, calls=%fused_computation.143 | loop fusion | flops 25878528 | bytes 31850496 | tf_op jit(solution)/shard_map/reshape.83
  184.8 8.2 copy.305
  198.9 10.8 %fusion = f32[3,4,4,8,385]{3,2,4,1,0:T(4,128)} fusion(f32[3,4,4,8,384]{3,2,4,1,0:T(4,128)} %bitcast.323, f32[3,4,4,8,384]{3,2,4,1,0:T(4,128)S(1)} %bitcast.319), kind=kLoop, calls=%fused_computation.4 | loop fusion | flops 147840 | bytes 1771008 | tf_op jit(solution)/shard_map/while/body/eval_jaxpr/add | solution.py:111
  223.7 9.2 copy.307
  262.2 8.0 copy.314
  270.3 10.3 %copy.315 = f32[3,4,4,8,128,3]{4,5,3,2,1,0:T(4,128)} copy(f32[3,4,4,8,128,3]{3,2,5,4,1,0:T(4,128)} %bitcast.327) | data formatting | bytes 1179648 | tf_op jit(solution)/shard_map/while/body/eval_jaxpr/reshape | solution.py:84
  320.0 8.2 copy.322
  328.2 12.8 %fusion.1 = f32[3,4,4,8,385]{3,2,4,1,0:T(4,128)} fusion(f32[3,4,4,8,384]{3,2,4,1,0:T(4,128)} %bitcast.320, f32[3,4,4,8,384]{3,2,4,1,0:T(4,128)} %bitcast.324), kind=kLoop, calls=%fused_computation.5 | loop fusion | flops 147840 | bytes 1771008 | tf_op jit(solution)/shard_map/while/body/eval_jaxpr/add | solution.py:111
  356.5 10.0 copy.324
  388.2 66.0 %all-reduce.36 = (f32[]{:T(128)}, f32[]{:T(128)}) all-reduce(f32[]{:T(128)} %get-tuple-element.88, f32[]{:T(128)} %get-tuple-element.87), channel_id=1, replica_groups=mesh['gx'=8,'gy'=16] {'gx','gy'}, use_global_device_ids=true, to_apply=%region_1.2 | all-reduce | flops 2 | bytes 16 | tf_op jit(solution)/shard_map/psum | solution.py:267
  457.2 62.5 %psum.44 = f32[]{:T(128)} all-reduce(f32[]{:T(128)} %get-tuple-element.114), channel_id=1, replica_groups=mesh['gx'=8,'gy'=16] {'gx','gy'}, use_global_device_ids=true, to_apply=%region_5.6 | all-reduce | flops 1 | bytes 8 | tf_op jit(solution)/shard_map/psum | solution.py:267
  536.6 8.0 copy.332
  544.6 10.3 %copy.333 = f32[3,4,4,8,128,3]{4,5,3,2,1,0:T(4,128)} copy(f32[3,4,4,8,128,3]{3,2,5,4,1,0:T(4,128)} %bitcast.328) | data formatting | bytes 1179648 | tf_op jit(solution)/shard_map/while/body/eval_jaxpr/reshape | solution.py:84
  554.9 8.5 slice.502
  596.9 8.2 copy.339
  605.0 12.8 %fusion.2 = f32[3,4,4,8,385]{3,2,4,1,0:T(4,128)} fusion(f32[3,4,4,8,384]{3,2,4,1,0:T(4,128)} %bitcast.321, f32[3,4,4,8,384]{3,2,4,1,0:T(4,128)} %bitcast.325), kind=kLoop, calls=%fused_computation.6 | loop fusion | flops 147840 | bytes 1771008 | tf_op jit(solution)/shard_map/while/body/eval_jaxpr/add | solution.py:111
  633.3 10.0 copy.341
  665.9 65.0 %psum.45 = f32[]{:T(128)} all-reduce(f32[]{:T(128)} %get-tuple-element.112), channel_id=1, replica_groups=mesh['gx'=8,'gy'=16] {'gx','gy'}, use_global_device_ids=true, to_apply=%region_7.8 | all-reduce | flops 1 | bytes 8 | tf_op jit(solution)/shard_map/psum | solution.py:267
  735.6 62.5 %psum.46 = f32[]{:T(128)} all-reduce(f32[]{:T(128)} %multiply_reduce_fusion), channel_id=1, replica_groups=mesh['gx'=8,'gy'=16] {'gx','gy'}, use_global_device_ids=true, to_apply=%region_9.10 | all-reduce | flops 1 | bytes 8 | tf_op jit(solution)/shard_map/psum | solution.py:267
  813.1 8.0 copy.349
  821.2 10.3 %copy.350 = f32[3,4,4,8,128,3]{4,5,3,2,1,0:T(4,128)} copy(f32[3,4,4,8,128,3]{3,2,5,4,1,0:T(4,128)} %bitcast.329) | data formatting | bytes 1179648 | tf_op jit(solution)/shard_map/while/body/eval_jaxpr/reshape | solution.py:84
  831.5 7.9 slice.527
  877.1 12.9 %fusion.3 = f32[3,4,4,8,385]{3,2,4,1,0:T(4,128)} fusion(f32[3,4,4,8,384]{3,2,4,1,0:T(4,128)} %bitcast.322, f32[3,4,4,8,384]{3,2,4,1,0:T(4,128)} %bitcast.326), kind=kLoop, calls=%fused_computation.7 | loop fusion | flops 147840 | bytes 1771008 | tf_op jit(solution)/shard_map/while/body/eval_jaxpr/add | solution.py:111
  905.4 9.1 copy.358
  933.3 65.1 %psum.47 = f32[]{:T(128)} all-reduce(f32[]{:T(128)} %fusion.140), channel_id=1, replica_groups=mesh['gx'=8,'gy'=16] {'gx','gy'}, use_global_device_ids=true, to_apply=%region_11.12 | all-reduce | flops 1 | bytes 8 | tf_op jit(solution)/shard_map/psum | solution.py:267
  (285 shorter events, 391.5 us)
Async XLA Ops:
  0.6 13.7 %copy-start.25 = (f32[6,3,1,1,1]{0,1,4,3,2:T(4,128)S(1)}, f32[6,3,1,1,1]{0,1,4,3,2:T(4,128)}, u32[]{:S(2)}) copy-start(f32[6,3,1,1,1]{0,1,4,3,2:T(4,128)} %constant.174) | copy-start | bytes 220
  2.7 6.7 collective-permute-start
  9.4 6.4 collective-permute-start.1
  33.9 33.5 %copy-start.18 = (f32[6,4,1,1,1,1]{0,1,5,4,3,2:T(4,128)S(1)}, f32[6,4,1,1,1,1]{0,1,5,4,3,2:T(4,128)}, u32[]{:S(2)}) copy-start(f32[6,4,1,1,1,1]{0,1,5,4,3,2:T(4,128)} %constant.172) | copy-start | bytes 292
  131.7 5.6 slice-start
  131.7 7.5 slice-start.2
  131.7 7.7 slice-start.1
  131.7 8.0 slice-start.3
  139.7 4.8 copy-start.1
  192.9 6.0 copy-start
  235.7 10.8 %copy-start.3 = (s32[3,3,24,384]{3,2,1,0:T(8,128)S(1)}, s32[3,3,24,384]{3,2,1,0:T(8,128)}, u32[]{:S(2)}) copy-start(s32[3,3,24,384]{3,2,1,0:T(8,128)} %param.12) | copy-start | bytes 995332
  235.8 18.2 %copy-start.2 = (f32[216,1,8,128]{3,2,1,0:T(8,128)S(1)}, f32[216,1,8,128]{3,2,1,0:T(8,128)}, u32[]{:S(2)}) copy-start(f32[216,1,8,128]{3,2,1,0:T(8,128)} %param.11) | copy-start | bytes 2654212
  235.8 6.0 collective-permute-start.2
  241.9 4.6 collective-permute-start.3
  246.6 5.5 collective-permute-start.4
  252.2 2.7 collective-permute-start.5
  376.8 6.3 collective-permute-start.6
  383.1 4.2 collective-permute-start.7
  387.4 66.8 %copy-start.22 = (f32[3,1,24,384]{3,2,1,0:T(8,128)}, f32[3,1,24,384]{3,2,1,0:T(8,128)S(1)}, u32[]{:S(2)}) copy-start(f32[3,1,24,384]{3,2,1,0:T(8,128)S(1)} %maximum_add_fusion.2) | copy-start | bytes 331780
  521.1 4.2 collective-permute-start.8
  525.3 3.2 collective-permute-start.9
  654.5 8.6 copy-start.26
  654.9 6.7 collective-permute-start.10
  661.7 3.5 collective-permute-start.11
  799.5 4.2 collective-permute-start.12
  803.7 3.9 collective-permute-start.13
  922.2 8.0 copy-start.24
  922.4 6.0 collective-permute-start.14
  923.4 9.2 copy-start.23
  923.4 76.3 %copy-start.19 = (f32[3,3,24,384]{3,2,1,0:T(8,128)S(1)}, f32[3,3,24,384]{3,2,1,0:T(8,128)}, u32[]{:S(2)}) copy-start(f32[3,3,24,384]{3,2,1,0:T(8,128)} %param.8) | copy-start | bytes 995332
  923.4 76.3 %copy-start.20 = (f32[3,3,24,384]{3,2,1,0:T(8,128)S(1)}, f32[3,3,24,384]{3,2,1,0:T(8,128)}, u32[]{:S(2)}) copy-start(f32[3,3,24,384]{3,2,1,0:T(8,128)} %param.9) | copy-start | bytes 995332
  928.4 3.5 collective-permute-start.15
  (16 other events, 34.7 us)
where the time goes:
time: 1010 us; the launch traced here: 1000 us
  local copies, waits for them, and re-layouts  364 us (36%)
  blocking collectives  321 us (32%)
  matrix products  153 us (15%)
  other arithmetic  88.8 us (9%)
  waiting for transfers between devices  40 us (4%)
  starting transfers between devices  25.2 us (2%)
    psum x5, blocking collectives, global_sum(): return lax.psum(value, ('gx', 'gy'))  321 us
    transpose x16, local copies, waits for them, and re-layouts, merge_nodes(): jnp.moveaxis(lax.slice_in_dim(operand, 0, 3, axis=which_axis), which_axis...  104 us
    dot_general x14, matrix products, along_x(): return jnp.einsum('qa,cabgjk->cqbgjk', matrix, operand, precision=HIGHEST)  55.3 us
    dot_general x15, matrix products, along_y(): return jnp.einsum('qb,cabgjk->caqgjk', matrix, operand, precision=HIGHEST)  50.4 us
    reshape x8, local copies, waits for them, and re-layouts, split_nodes(): lax.slice_in_dim(operand, 0, 3 * num_cells, axis=which_axis)  50.1 us
    add x12, other arithmetic, merge_nodes(): return jnp.pad(head_part, pad_head) + shifted  50 us
    dot_general x14, matrix products, along_z(): return jnp.einsum('qg,cabgjk->cabqjk', matrix, operand, precision=HIGHEST)  47.1 us
    slice x8, local copies, waits for them, and re-layouts, split_nodes(): lax.slice_in_dim(operand, 3, 3 * num_cells + 1, stride=3, axis=which_axis)  46.5 us
  transfers between devices with their start and end apart: 16, of which 13 were waited for; matrix products, arithmetic and copies ran while one was open for 1% of the time, Pallas kernels for 0%

commit v1 on v0

--- a/solution.py
+++ b/solution.py
@@ -264,7 +264,7 @@
 
 
 def global_sum(value):
-    return lax.psum(value, ("gx", "gy"))
+    return lax.psum(lax.psum(value, "gx"), "gy")
 
 
 def on_device(displacement, velocity, energy, mass_weight, pinned_flags):

time: 1010 us -> 958 us (0.949)
  blocking collectives: 321 us -> 242 us
  starting transfers between devices: 25.2 us -> 37.1 us
    psum x5 -> x10, blocking collectives: 321 us -> 242 us  [global_sum(): return lax.psum(lax.psum(value, 'gx'), 'gy')]
    ppermute x16, starting transfers between devices: 25.2 us -> 37.1 us  [shifted_2(): lax.ppermute(shard, axis, [(i, (i + by) % devices) for i in range(devices)])]
    unnamed x73 -> x81, local copies, waits for them, and re-layouts: 39.7 us -> 42.1 us
where the time goes in v1:
time: 958 us; the launch traced here: 939 us
  local copies, waits for them, and re-layouts  366 us (38%)
  blocking collectives  242 us (25%)
  matrix products  154 us (16%)
  other arithmetic  92.9 us (10%)
  waiting for transfers between devices  38.5 us (4%)
  starting transfers between devices  37.1 us (4%)
    psum x10, blocking collectives, global_sum(): return lax.psum(lax.psum(value, 'gx'), 'gy')  242 us
    transpose x16, local copies, waits for them, and re-layouts, merge_nodes(): jnp.moveaxis(lax.slice_in_dim(operand, 0, 3, axis=which_axis), which_axis...  102 us
    dot_general x14, matrix products, along_x(): return jnp.einsum('qa,cabgjk->cqbgjk', matrix, operand, precision=HIGHEST)  56.4 us
    dot_general x15, matrix products, along_y(): return jnp.einsum('qb,cabgjk->caqgjk', matrix, operand, precision=HIGHEST)  50.7 us
    reshape x8, local copies, waits for them, and re-layouts, split_nodes(): lax.slice_in_dim(operand, 0, 3 * num_cells, axis=which_axis)  50.1 us
    add x12, other arithmetic, merge_nodes(): return jnp.pad(head_part, pad_head) + shifted  49.9 us
    dot_general x14, matrix products, along_z(): return jnp.einsum('qg,cabgjk->cabqjk', matrix, operand, precision=HIGHEST)  47.3 us
    slice x8, local copies, waits for them, and re-layouts, split_nodes(): lax.slice_in_dim(operand, 3, 3 * num_cells + 1, stride=3, axis=which_axis)  46 us
  transfers between devices with their start and end apart: 16, of which 13 were waited for; matrix products, arithmetic and copies ran while one was open for 1% of the time, Pallas kernels for 0%

profile of v1, /device:TPU:1, one launch (start us, length us, event | category | flops | bytes accessed | tf_op | source)
XLA Modules:
  0.0 939.2 jit_solution(8791267213750315366)
XLA Ops:
  20.2 12.5 %copy.282 = f32[6,4,4,8,384]{3,2,4,1,0:T(4,128)} copy(f32[6,4,4,8,384]{4,3,2,1,0:T(8,128)S(1)} %fusion.109) | data formatting | bytes 2359296 | tf_op jit(solution)/shard_map/while/body/eval_jaxpr/slice | solution.py:84
  32.7 18.3 %copy.283 = f32[6,4,4,8,128,3]{4,5,3,2,1,0:T(4,128)S(1)} copy(f32[6,4,4,8,128,3]{3,2,5,4,1,0:T(4,128)} %bitcast.311) | data formatting | bytes 2359296 | tf_op jit(solution)/shard_map/while/body/eval_jaxpr/reshape | solution.py:84
  51.0 15.0 %slice.434 = f32[6,4,4,8,128]{4,3,2,1,0:T(8,128)S(1)} slice(f32[6,4,4,8,385]{4,3,2,1,0:T(8,128)} %pad_maximum_fusion.3), slice={[0:6:1], [0:4:1], [0:4:1], [0:8:1], [3:385:3]} | slice | bytes 786432 | tf_op jit(solution)/shard_map/while/body/eval_jaxpr/slice | solution.py:88
  85.0 9.3 fusion.18
  100.0 9.4 %fusion.16 = f32[6,6,6,8,128,6]{4,5,3,2,1,0:T(8,128)} fusion(f32[6,4,1,1,1,1]{0,1,5,4,3,2:T(4,128)S(1)} %copy-done.22, f32[6,4,6,6,8,128]{5,2,4,3,1,0:T(8,128)S(1)} %fusion.36), kind=kOutput, calls=%fused_computation.30 | convolution fusion | flops 63700992 | bytes 8847456 | tf_op jit(solution)/shard_map/while/body/eval_jaxpr/qa,cabgjk->cqbgjk/dot_general | solution.py:69
  109.4 9.5 %fusion.20 = f32[6,6,6,8,128,6]{4,5,3,2,1,0:T(8,128)S(1)} fusion(f32[6,4,1,1,1,1]{0,1,5,4,3,2:T(4,128)S(1)} %copy-done.31, f32[6,4,6,6,8,128]{5,2,4,3,1,0:T(8,128)S(1)} %convolution_bitcast_fusion.1), kind=kOutput, calls=%fused_computation.34 | convolution fusion | flops 63700992 | bytes 8847456 | tf_op jit(solution)/shard_map/while/body/eval_jaxpr/qa,cabgjk->cqbgjk/dot_general | solution.py:69
  119.8 10.7 %copy_bitcast_fusion = (f32[6,6,6,6,8,128]{5,4,3,2,1,0:T(8,128)}, f32[6,6,6,6,8,128]{5,4,3,2,1,0:T(8,128)}) fusion(f32[6,6,6,8,128,6]{4,5,3,2,1,0:T(8,128)} %fusion.16, f32[6,6,6,8,128,6]{4,5,3,2,1,0:T(8,128)} %fusion.18), kind=kLoop, calls=%fused_computation.12 | loop fusion | bytes 21233664 | tf_op jit(solution)/shard_map/while/body/eval_jaxpr/qa,cabgjk->cqbgjk/transpose | solution.py:69
  144.1 11.7 %add_bitcast_fusion = (f32[6,6,6,8,128]{4,3,2,1,0:T(8,128)}, f32[1,6,6,6,8,128]{5,4,3,2,1,0:T(8,128)}, f32[1,6,6,6,8,128]{5,4,3,2,1,0:T(8,128)}, f32[1,6,6,6,8,1...) fusion(f32[1,6,6,6,8,128]{5,4,3,2,1,0:T(8,128)} %get-tuple-elem, ...), kind=kLoop, calls=%fused_computation.143 | loop fusion | flops 25878528 | bytes 31850496 | tf_op jit(solution)/shard_map/reshape.83
  200.5 10.8 %fusion = f32[3,4,4,8,385]{3,2,4,1,0:T(4,128)} fusion(f32[3,4,4,8,384]{3,2,4,1,0:T(4,128)} %bitcast.323, f32[3,4,4,8,384]{3,2,4,1,0:T(4,128)S(1)} %bitcast.319), kind=kLoop, calls=%fused_computation.4 | loop fusion | flops 147840 | bytes 1771008 | tf_op jit(solution)/shard_map/while/body/eval_jaxpr/add | solution.py:111
  225.3 9.2 copy.307
  272.9 10.3 %copy.315 = f32[3,4,4,8,128,3]{4,5,3,2,1,0:T(4,128)} copy(f32[3,4,4,8,128,3]{3,2,5,4,1,0:T(4,128)} %bitcast.327) | data formatting | bytes 1179648 | tf_op jit(solution)/shard_map/while/body/eval_jaxpr/reshape | solution.py:84
  322.6 8.3 copy.322
  331.0 12.8 %fusion.1 = f32[3,4,4,8,385]{3,2,4,1,0:T(4,128)} fusion(f32[3,4,4,8,384]{3,2,4,1,0:T(4,128)} %bitcast.320, f32[3,4,4,8,384]{3,2,4,1,0:T(4,128)} %bitcast.324), kind=kLoop, calls=%fused_computation.5 | loop fusion | flops 147840 | bytes 1771008 | tf_op jit(solution)/shard_map/while/body/eval_jaxpr/add | solution.py:111
  359.3 10.0 %copy.324 = f32[3,4,8,3,385]{4,1,3,2,0:T(4,128)} copy(f32[3,4,8,3,385]{2,3,4,1,0:T(4,128)} %slice_bitcast_fusion.2) | data formatting | bytes 887040 | tf_op jit(solution)/shard_map/while/body/eval_jaxpr/transpose | solution.py:96
  391.0 17.0 %all-reduce.37 = (f32[]{:T(128)}, f32[]{:T(128)}) all-reduce(f32[]{:T(128)} %get-tuple-element.88, f32[]{:T(128)} %get-tuple-element.87), channel_id=1, replica_groups=mesh['gx'=8,'gy'=16] {'gx'}, use_global_device_ids=true, to_apply=%region_1.2 | all-reduce | flops 2 | bytes 16 | tf_op jit(solution)/shard_map/psum | solution.py:267
  408.0 30.4 %all-reduce.36 = (f32[]{:T(128)}, f32[]{:T(128)}) all-reduce(f32[]{:T(128)} %get-tuple-element.96, f32[]{:T(128)} %get-tuple-element.97), channel_id=1, replica_groups=mesh['gx'=8,'gy'=16] {'gy'}, use_global_device_ids=true, to_apply=%region_2.3 | all-reduce | flops 2 | bytes 16 | tf_op jit(solution)/shard_map/psum | solution.py:267
  441.3 20.2 %psum.88 = f32[]{:T(128)} all-reduce(f32[]{:T(128)} %get-tuple-element.116), channel_id=1, replica_groups=mesh['gx'=8,'gy'=16] {'gx'}, use_global_device_ids=true, to_apply=%region_7.8 | all-reduce | flops 1 | bytes 8 | tf_op jit(solution)/shard_map/psum | solution.py:267
  461.5 29.5 %psum.89 = f32[]{:T(128)} all-reduce(f32[]{:T(128)} %psum.88), channel_id=1, replica_groups=mesh['gx'=8,'gy'=16] {'gy'}, use_global_device_ids=true, to_apply=%region_8.9 | all-reduce | flops 1 | bytes 8 | tf_op jit(solution)/shard_map/psum | solution.py:267
  520.0 10.3 %copy.333 = f32[3,4,4,8,128,3]{4,5,3,2,1,0:T(4,128)} copy(f32[3,4,4,8,128,3]{3,2,5,4,1,0:T(4,128)} %bitcast.328) | data formatting | bytes 1179648 | tf_op jit(solution)/shard_map/while/body/eval_jaxpr/reshape | solution.py:84
  530.2 8.5 slice.502
  572.1 8.3 copy.339
  580.4 12.8 %fusion.2 = f32[3,4,4,8,385]{3,2,4,1,0:T(4,128)} fusion(f32[3,4,4,8,384]{3,2,4,1,0:T(4,128)} %bitcast.321, f32[3,4,4,8,384]{3,2,4,1,0:T(4,128)} %bitcast.325), kind=kLoop, calls=%fused_computation.6 | loop fusion | flops 147840 | bytes 1771008 | tf_op jit(solution)/shard_map/while/body/eval_jaxpr/add | solution.py:111
  608.7 10.0 %copy.341 = f32[3,4,8,3,385]{4,1,3,2,0:T(4,128)} copy(f32[3,4,8,3,385]{2,3,4,1,0:T(4,128)} %slice_bitcast_fusion.1) | data formatting | bytes 887040 | tf_op jit(solution)/shard_map/while/body/eval_jaxpr/transpose | solution.py:96
  642.3 17.0 %psum.90 = f32[]{:T(128)} all-reduce(f32[]{:T(128)} %get-tuple-element.114), channel_id=1, replica_groups=mesh['gx'=8,'gy'=16] {'gx'}, use_global_device_ids=true, to_apply=%region_10.11 | all-reduce | flops 1 | bytes 8 | tf_op jit(solution)/shard_map/psum | solution.py:267
  659.3 30.4 %psum.91 = f32[]{:T(128)} all-reduce(f32[]{:T(128)} %psum.90), channel_id=1, replica_groups=mesh['gx'=8,'gy'=16] {'gy'}, use_global_device_ids=true, to_apply=%region_11.12 | all-reduce | flops 1 | bytes 8 | tf_op jit(solution)/shard_map/psum | solution.py:267
  694.7 20.2 %psum.92 = f32[]{:T(128)} all-reduce(f32[]{:T(128)} %multiply_reduce_fusion), channel_id=1, replica_groups=mesh['gx'=8,'gy'=16] {'gx'}, use_global_device_ids=true, to_apply=%region_13.14 | all-reduce | flops 1 | bytes 8 | tf_op jit(solution)/shard_map/psum | solution.py:267
  717.6 29.5 %psum.93 = f32[]{:T(128)} all-reduce(f32[]{:T(128)} %psum.92), channel_id=1, replica_groups=mesh['gx'=8,'gy'=16] {'gy'}, use_global_device_ids=true, to_apply=%region_14.15 | all-reduce | flops 1 | bytes 8 | tf_op jit(solution)/shard_map/psum | solution.py:267
  776.1 10.3 %copy.350 = f32[3,4,4,8,128,3]{4,5,3,2,1,0:T(4,128)} copy(f32[3,4,4,8,128,3]{3,2,5,4,1,0:T(4,128)} %bitcast.329) | data formatting | bytes 1179648 | tf_op jit(solution)/shard_map/while/body/eval_jaxpr/reshape | solution.py:84
  832.0 12.8 %fusion.3 = f32[3,4,4,8,385]{3,2,4,1,0:T(4,128)} fusion(f32[3,4,4,8,384]{3,2,4,1,0:T(4,128)} %bitcast.322, f32[3,4,4,8,384]{3,2,4,1,0:T(4,128)} %bitcast.326), kind=kLoop, calls=%fused_computation.7 | loop fusion | flops 147840 | bytes 1771008 | tf_op jit(solution)/shard_map/while/body/eval_jaxpr/add | solution.py:111
  860.3 9.1 copy.358
  888.5 17.0 %psum.94 = f32[]{:T(128)} all-reduce(f32[]{:T(128)} %fusion.140), channel_id=1, replica_groups=mesh['gx'=8,'gy'=16] {'gx'}, use_global_device_ids=true, to_apply=%region_16.17 | all-reduce | flops 1 | bytes 8 | tf_op jit(solution)/shard_map/psum | solution.py:267
  906.2 30.4 %psum.95 = f32[]{:T(128)} all-reduce(f32[]{:T(128)} %psum.94), channel_id=1, replica_groups=mesh['gx'=8,'gy'=16] {'gy'}, use_global_device_ids=true, to_apply=%region_17.18 | all-reduce | flops 1 | bytes 8 | tf_op jit(solution)/shard_map/psum | solution.py:267
  (298 shorter events, 448.9 us)
Async XLA Ops:
  0.6 13.7 %copy-start.29 = (f32[6,3,1,1,1]{0,1,4,3,2:T(4,128)S(1)}, f32[6,3,1,1,1]{0,1,4,3,2:T(4,128)}, u32[]{:S(2)}) copy-start(f32[6,3,1,1,1]{0,1,4,3,2:T(4,128)} %constant.174) | copy-start | bytes 220
  2.7 6.7 collective-permute-start
  9.4 7.5 collective-permute-start.1
  32.7 33.3 %copy-start.22 = (f32[6,4,1,1,1,1]{0,1,5,4,3,2:T(4,128)S(1)}, f32[6,4,1,1,1,1]{0,1,5,4,3,2:T(4,128)}, u32[]{:S(2)}) copy-start(f32[6,4,1,1,1,1]{0,1,5,4,3,2:T(4,128)} %constant.172) | copy-start | bytes 292
  130.6 5.9 slice-start
  130.6 7.8 slice-start.2
  130.6 8.0 slice-start.1
  130.6 8.3 slice-start.3
  144.1 11.7 %copy-start.5 = (f32[1,6,6,6,8,128]{5,4,3,2,1,0:T(8,128)S(1)}, f32[1,6,6,6,8,128]{5,4,3,2,1,0:T(8,128)}, u32[]{:S(2)}) copy-start(f32[1,6,6,6,8,128]{5,4,3,2,1,0:T(8,128)} %get-tuple-element.127) | copy-start | bytes 2654212
  192.8 7.7 copy-start
  238.9 10.3 %copy-start.4 = (s32[3,3,24,384]{3,2,1,0:T(8,128)S(1)}, s32[3,3,24,384]{3,2,1,0:T(8,128)}, u32[]{:S(2)}) copy-start(s32[3,3,24,384]{3,2,1,0:T(8,128)} %param.12) | copy-start | bytes 995332
  239.0 17.1 %copy-start.3 = (f32[216,1,8,128]{3,2,1,0:T(8,128)S(1)}, f32[216,1,8,128]{3,2,1,0:T(8,128)}, u32[]{:S(2)}) copy-start(f32[216,1,8,128]{3,2,1,0:T(8,128)} %param.11) | copy-start | bytes 2654212
  239.0 6.0 collective-permute-start.2
  245.1 4.1 collective-permute-start.3
  249.2 5.5 collective-permute-start.4
  254.8 2.7 collective-permute-start.5
  379.6 6.0 collective-permute-start.6
  385.7 4.5 collective-permute-start.7
  390.2 48.1 %copy-start.26 = (f32[3,1,24,384]{3,2,1,0:T(8,128)}, f32[3,1,24,384]{3,2,1,0:T(8,128)S(1)}, u32[]{:S(2)}) copy-start(f32[3,1,24,384]{3,2,1,0:T(8,128)S(1)} %maximum_add_fusion.2) | copy-start | bytes 331780
  492.5 8.7 collective-permute-start.8
  501.2 2.7 collective-permute-start.9
  630.3 62.4 %copy-start.30 = (f32[6,3,1,1,1]{0,1,4,3,2:T(4,128)S(1)}, f32[6,3,1,1,1]{0,1,4,3,2:T(4,128)}, u32[]{:S(2)}) copy-start(f32[6,3,1,1,1]{0,1,4,3,2:T(4,128)} %constant.174) | copy-start | bytes 220
  630.3 6.0 collective-permute-start.10
  636.4 4.5 collective-permute-start.11
  749.5 10.1 %collective-permute-start.12 = (f32[3,1,24,384]{3,2,1,0:T(8,128)S(1)}, f32[3,1,24,384]{3,2,1,0:T(8,128)S(1)}, u32[]{:S(2)}, u32[]{:S(2)}) collective-permute-start(f32[3,1,24,384]{3,2,1,0:T(8,128)S(1)} %slice.612), channel_id=1, source_target_pairs={{0,112},{16,0},{32,16},{48,32},{64,48},{80,64},{96,80},{112,96},{1... | collective-permute-start | bytes 331784 | tf_op jit(solution)/shard_map/ppermute | solution.py:19
  759.7 2.9 collective-permute-start.13
  878.7 6.5 copy-start.28
  878.8 6.0 collective-permute-start.14
  880.4 25.1 %copy-start.27 = (f32[27,1,8,128]{3,2,1,0:T(8,128)S(1)}, f32[27,1,8,128]{3,2,1,0:T(8,128)}, u32[]{:S(2)}) copy-start(f32[27,1,8,128]{3,2,1,0:T(8,128)} %param.10) | copy-start | bytes 331780
  880.4 57.5 %copy-start.23 = (f32[3,3,24,384]{3,2,1,0:T(8,128)S(1)}, f32[3,3,24,384]{3,2,1,0:T(8,128)}, u32[]{:S(2)}) copy-start(f32[3,3,24,384]{3,2,1,0:T(8,128)} %param.8) | copy-start | bytes 995332
  880.4 57.5 %copy-start.24 = (f32[3,3,24,384]{3,2,1,0:T(8,128)S(1)}, f32[3,3,24,384]{3,2,1,0:T(8,128)}, u32[]{:S(2)}) copy-start(f32[3,3,24,384]{3,2,1,0:T(8,128)} %param.9) | copy-start | bytes 995332
  884.9 2.9 collective-permute-start.15
  (20 other events, 48.2 us)
